TPU v7x, 32 devices: a whole 2x2x4 slice. The times are simulated.
32 devices in a mesh: space: 16 (over z, y, core), mem: 2 (over x).
Axes of the slice: x: 2, y: 2, z: 4, core: 2. Of those that a mesh axis runs over, the one named last changes fastest.
Arguments:
- member_heat_solute: float32 [128, 2, 256, 128], P('mem', None, 'space'), may hold values from -6 to 6
- velocity: float32 [128, 256, 128], P('mem', 'space'), may hold values from 0.2 to 0.6
- phase_mask: int32 [256, 128], P('space'), may hold values 0 or 1
- obs_index: int32 [256], P('space'), may hold values from 0 to 2047
- obs_value: float32 [256], P('space'), may hold values from -6 to 6
- obs_error: float32 [256], P('space'), may hold values from 0.3 to 3
Outputs:
- analysis_hc: float32 [128, 2, 256, 128], P('mem', None, 'space')
- analysis_velocity: float32 [128, 256, 128], P('mem', 'space')
Inputs may be any that keep to these rules, and one draw needn't show every extreme that they name: `obs_index`: observation o lies in slab o // 16; its entry counts cells row by row inside that slab.
All inputs are finite; a program needn't handle non-finite values. No bound on the sum of `phase_mask` on one device may be relied on, other than what follows from the above.
Results may differ from a plain program's by a relative error of at most 0.00015.
Values sent between devices are 32-bit elements; how exact they have to be, the bound alone decides.
A program may use at most 64 MiB of HBM per device.

v0:
```python
import functools

import jax
import jax.numpy as jnp
from jax import lax
from jax.experimental import pallas as pl
from jax.experimental.pallas import tpu as pltpu
from jax.sharding import PartitionSpec as P

heat_diffusion = 0.15
advection = 0.4
solute_diffusion = 0.05
segregation = 0.3
momentum_diffusion = 0.1
darcy_drag = 0.5
mushy_ratio = 1.0 / 3.0

MESH = pl.DeviceIdType.MESH
HIGHEST = lax.Precision.HIGHEST
HEAT, SOLUTE, SPEED = 0, 1, 2
PANEL = 16


def lateral_sum(field):
    lane = lax.broadcasted_iota(jnp.int32, field.shape, 2)
    last = field.shape[2] - 1
    left = jnp.where(lane == 0, field, pltpu.roll(field, 1, 2))
    right = jnp.where(lane == last, field, pltpu.roll(field, last, 2))
    return left + right


def laplacian(field):
    centre = field[1:-1]
    return field[2:] + field[:-2] + lateral_sum(centre) - 4.0 * centre


def advance_speed(speed, mushy):
    centre = speed[1:-1]
    return centre + momentum_diffusion * laplacian(speed) - darcy_drag * mushy[1:-1] * centre


def advance_pair(heat, solute, speed, mushy):
    temp = heat * (1.0 - mushy * (1.0 - mushy_ratio))
    drift = advection * speed[1:-1]
    new_heat = (
        heat[1:-1] + heat_diffusion * laplacian(temp) - drift * (heat[1:-1] - heat[:-2])
    )
    new_solute = (
        solute[1:-1]
        + solute_diffusion * laplacian(solute)
        - drift * (solute[1:-1] - solute[:-2])
        + segregation * mushy[1:-1] * (temp[1:-1] - solute[1:-1])
    )
    return new_heat, new_solute


def split(values):
    high = values.astype(jnp.bfloat16)
    low = (values - high.astype(jnp.float32)).astype(jnp.bfloat16)
    return high, low


def split_three(values):
    parts = []
    for _ in range(3):
        part = values.astype(jnp.bfloat16).astype(jnp.float32)
        parts.append(part)
        values = values - part
    return parts


def inverse_factor(matrix_ref):
    order = matrix_ref.shape[0]
    lane = lax.broadcasted_iota(jnp.int32, (PANEL, order), 1)
    sub = lax.broadcasted_iota(jnp.int32, (PANEL, order), 0)
    rows = lax.broadcasted_iota(jnp.int32, (order, order), 0)
    lanes = lax.broadcasted_iota(jnp.int32, (order, order), 1)

    def panel(block, carry):
        base = pl.multiple_of(block * PANEL, PANEL)
        here = matrix_ref[pl.ds(base, PANEL), :]
        cols = [
            jnp.broadcast_to(
                jnp.sum(jnp.where(lane == base + s, here, 0.0), axis=1, keepdims=True),
                (PANEL, order),
            )
            for s in range(PANEL)
        ]
        upper = jnp.where(lane >= base, here, 0.0)
        inverse = jnp.where(lane < base, here, jnp.where(lane == base + sub, 1.0, 0.0))
        diagonal = jnp.zeros((PANEL, order), jnp.float32)
        for s in range(PANEL):
            pivot = cols[s][s : s + 1]
            diagonal = jnp.where(sub == s, pivot, diagonal)
            factor = jnp.where(sub > s, cols[s] / pivot, 0.0)
            upper = upper - factor * upper[s : s + 1]
            inverse = inverse - factor * inverse[s : s + 1]
            for t in range(s + 1, PANEL):
                cols[t] = cols[t] - factor * cols[t][s : s + 1]
        scale = 1.0 / jnp.sqrt(diagonal)
        upper = upper * scale
        inverse = inverse * scale
        right = jnp.where(lane < base + PANEL, inverse, upper)
        upper_parts = split_three(upper)
        right_parts = split_three(right)
        change = lax.dot_general(
            jnp.concatenate([upper_parts[i] for i in (0, 0, 1, 1, 0, 2)], axis=0).astype(jnp.bfloat16),
            jnp.concatenate([right_parts[i] for i in (0, 1, 0, 1, 2, 0)], axis=0).astype(jnp.bfloat16),
            (((0,), (0,)), ((), ())),
            preferred_element_type=jnp.float32,
        )
        old = matrix_ref[...]
        kept = jnp.where((lanes >= base) & (lanes < base + PANEL), 0.0, old)
        matrix_ref[...] = jnp.where(rows >= base + PANEL, kept - change, old)
        matrix_ref[pl.ds(base, PANEL), :] = inverse
        return carry

    lax.fori_loop(0, order // PANEL, panel, 0)


def kernel(
    slabs, halves,
    hc_ref, v_ref, phase_ref, cell_ref, datum_ref, deviate_ref,
    out_hc_ref, out_v_ref,
    mask_ref, index_ref, value_ref, error_ref, hc, vel, raw, mushy, own, other, sums, seen, square,
    in_sem, halo_send, halo_recv, state_send, state_recv, seen_send, seen_recv, sum_send, sum_recv,
):
    members = own.shape[2]
    width = own.shape[3]
    depth = own.shape[1]
    groups = members // 8
    everyone = slabs * halves
    ens = members * halves
    slab = lax.axis_index("space")
    half = lax.axis_index("mem")
    me = slab * halves + half
    first = slab == 0
    last = slab == slabs - 1

    load_v = pltpu.make_async_copy(v_ref, vel, in_sem.at[0])
    load_hc = pltpu.make_async_copy(hc_ref, hc, in_sem.at[1])
    load_mask = pltpu.make_async_copy(phase_ref, mask_ref, in_sem.at[2])
    load_observed = [
        pltpu.make_async_copy(cell_ref, index_ref, in_sem.at[3]),
        pltpu.make_async_copy(datum_ref, value_ref, in_sem.at[4]),
        pltpu.make_async_copy(deviate_ref, error_ref, in_sem.at[5]),
    ]
    load_mask.start()
    load_v.start()
    load_hc.start()
    for load in load_observed:
        load.start()

    barrier = pltpu.get_barrier_semaphore()

    def greet(step, carry):
        peer = lax.rem(me + step, everyone)
        pl.semaphore_signal(
            barrier, inc=1, device_id=(peer // halves, lax.rem(peer, halves)), device_id_type=MESH
        )
        return carry

    lax.fori_loop(1, everyone, greet, 0)

    load_mask.wait()
    for z in range(depth):
        row = mask_ref[z : z + 1, :].astype(jnp.float32)
        mushy[z + 2] = jnp.broadcast_to(row, (8, width))

    def relayout_speed(zs):
        for z in zs:
            raw[SPEED, z + 2] = vel[pl.ds(z, members, stride=depth), :]

    def relayout_pair(zs):
        for z in zs:
            raw[HEAT, z + 2] = hc[pl.ds(z, members, stride=2 * depth), :]
            raw[SOLUTE, z + 2] = hc[pl.ds(depth + z, members, stride=2 * depth), :]

    load_v.wait()
    relayout_speed(range(depth))

    def inner_speed(group, carry):
        at = pl.ds(pl.multiple_of(group * 8, 8), 8)
        mask = mushy[2 : depth + 2]
        speed = advance_speed(raw[SPEED, 2 : depth + 2, at, :], mask)
        own[SPEED, 2 : depth - 2, at, :] = advance_speed(speed, mask[1:-1])
        return carry

    lax.fori_loop(0, groups, inner_speed, 0)
    load_hc.wait()
    relayout_pair((0, 1, depth - 2, depth - 1))

    def halo(direction, source, target, to, part):
        ref = raw if part == 0 else mushy
        pick = (lambda r, a: r.at[:, pl.ds(a, 2)]) if part == 0 else (lambda r, a: r.at[pl.ds(a, 2)])
        return pltpu.make_async_remote_copy(
            src_ref=pick(ref, source),
            dst_ref=pick(ref, target),
            send_sem=halo_send.at[direction, part],
            recv_sem=halo_recv.at[direction, part],
            device_id=(to, half),
            device_id_type=MESH,
        )

    up = [halo(0, 2, depth + 2, lax.rem(slab + slabs - 1, slabs), part) for part in range(2)]
    down = [halo(1, depth, 0, lax.rem(slab + 1, slabs), part) for part in range(2)]

    @pl.when(first)
    def _():
        raw[:, 0:2] = jnp.zeros((3, 2, members, width), jnp.float32)
        mushy[0:2] = jnp.zeros((2, 8, width), jnp.float32)

    @pl.when(last)
    def _():
        raw[:, depth + 2 : depth + 4] = jnp.zeros((3, 2, members, width), jnp.float32)
        mushy[depth + 2 : depth + 4] = jnp.zeros((2, 8, width), jnp.float32)

    pl.semaphore_wait(barrier, everyone - 1)

    @pl.when(jnp.logical_not(first))
    def _():
        for copy in up:
            copy.start()

    @pl.when(jnp.logical_not(last))
    def _():
        for copy in down:
            copy.start()

    pieces = []

    def send(field, start, count):
        number = len(pieces)
        copies = []
        for hop in range(1, halves):
            copies.append(
                pltpu.make_async_remote_copy(
                    src_ref=own.at[field, pl.ds(start, count)],
                    dst_ref=other.at[hop - 1, field, pl.ds(start, count)],
                    send_sem=state_send.at[hop - 1, number],
                    recv_sem=state_recv.at[hop - 1, number],
                    device_id=(slab, lax.rem(half + hop, halves)),
                    device_id_type=MESH,
                )
            )
        for hop, copy in enumerate(copies, 1):
            pl.when(half + hop < halves)(copy.start)
        pieces.append((field, start, count, copies))

    middle = depth // 2
    for z in range(2, depth - 2, 2):
        send(SPEED, z, 2)
    relayout_pair(range(2, depth - 2))

    def inner_pair(group, carry):
        at = pl.ds(pl.multiple_of(group * 8, 8), 8)
        mask = mushy[2 : depth + 2]
        before = raw[SPEED, 2 : depth + 2, at, :]
        heat, solute = advance_pair(
            raw[HEAT, 2 : depth + 2, at, :], raw[SOLUTE, 2 : depth + 2, at, :], before, mask
        )
        heat, solute = advance_pair(heat, solute, advance_speed(before, mask), mask[1:-1])
        own[HEAT, 2 : depth - 2, at, :] = heat
        own[SOLUTE, 2 : depth - 2, at, :] = solute
        return carry

    lax.fori_loop(0, groups, inner_pair, 0)
    for z in range(2, middle, 2):
        send(HEAT, z, 2)

    @pl.when(jnp.logical_not(last))
    def _():
        for copy in up:
            copy.wait_recv()

    @pl.when(jnp.logical_not(first))
    def _():
        for copy in down:
            copy.wait_recv()

    def edges(group, carry):
        at = pl.ds(pl.multiple_of(group * 8, 8), 8)
        for begin, outside, edge in ((0, first, 0), (depth - 2, last, 3)):
            mask = mushy[begin : begin + 6]
            before = raw[SPEED, begin : begin + 6, at, :]
            heat, solute = advance_pair(
                raw[HEAT, begin : begin + 6, at, :], raw[SOLUTE, begin : begin + 6, at, :], before, mask
            )
            speed = advance_speed(before, mask)
            row = lax.broadcasted_iota(jnp.int32, heat.shape, 0)
            beyond = jnp.logical_and(row == edge, outside)
            heat, solute, speed = [jnp.where(beyond, 0.0, q) for q in (heat, solute, speed)]
            mask = mask[1:-1]
            new_heat, new_solute = advance_pair(heat, solute, speed, mask)
            own[HEAT, begin : begin + 2, at, :] = new_heat
            own[SOLUTE, begin : begin + 2, at, :] = new_solute
            own[SPEED, begin : begin + 2, at, :] = advance_speed(speed, mask)
        return carry

    lax.fori_loop(0, groups, edges, 0)

    lane = lax.broadcasted_iota(jnp.int32, (members, width), 1)
    per_slab = index_ref.shape[0]
    for load in load_observed:
        load.wait()
    observed = jnp.zeros((members, width), jnp.float32)
    value = jnp.zeros((members, width), jnp.float32)
    error = jnp.ones((members, width), jnp.float32)
    for o in range(per_slab):
        cell = index_ref[o]
        z = cell // width
        w = cell - z * width
        factor = 1.0 - mushy[z + 2][0:1] * (1.0 - mushy_ratio)
        temp = jnp.where(lane == w, own[HEAT, z] * factor, 0.0)
        observed = jnp.where(lane == o, jnp.sum(temp, axis=1, keepdims=True), observed)
        value = jnp.where(lane == o, value_ref[o], value)
        error = jnp.where(lane == o, error_ref[o], error)
    square[...] = jnp.zeros((ens, width), jnp.float32)
    square[pl.ds(pl.multiple_of(half * members, 8), members), :] = (observed - value) / error
    turned = square[...].T
    seen[me] = turned[0:8] + pltpu.roll(turned[8:16], ens // 2, 1)

    def tell_copy(peer):
        return pltpu.make_async_remote_copy(
            src_ref=seen.at[me],
            dst_ref=seen.at[me],
            send_sem=seen_send.at[0],
            recv_sem=seen_recv.at[0],
            device_id=(peer // halves, lax.rem(peer, halves)),
            device_id_type=MESH,
        )

    def tell(step, carry):
        tell_copy(lax.rem(me + step, everyone)).start()
        return carry

    lax.fori_loop(1, everyone, tell, 0)

    for z in (0, depth - 2):
        send(SPEED, z, 2)
    for z in (0, *range(middle, depth, 2)):
        send(HEAT, z, 2)
    for z in range(0, depth, 2):
        send(SOLUTE, z, 2)

    for hop in range(1, halves):

        @pl.when(half < hop)
        def _():
            other[hop - 1, :, :, 8:, :] = jnp.zeros((3, depth, members - 8, width), jnp.float32)

    rest = seen.at[pl.ds(0, everyone - 1)]
    pltpu.make_async_copy(rest, rest, seen_recv.at[0]).wait()

    got = seen[...].reshape(slabs, halves, 8, ens)
    place = lax.broadcasted_iota(jnp.int32, (slabs, 8, ens), 2)
    low = jnp.zeros((slabs, 8, ens), jnp.float32)
    high = jnp.zeros((slabs, 8, ens), jnp.float32)
    for m in range(halves):
        mine = (place >= m * members) & (place < (m + 1) * members)
        low = jnp.where(mine, got[:, m], low)
        high = jnp.where(mine, pltpu.roll(got[:, m], ens // 2, 2), high)
    deviation = jnp.concatenate(
        [low.reshape(slabs * 8, ens), high.reshape(slabs * 8, ens)], axis=0
    )
    mean = jnp.sum(deviation, axis=1, keepdims=True) * (1.0 / ens)
    root = 1.0 / (ens - 1.0) ** 0.5
    spread = (deviation - mean) * root
    project = -jnp.sum(spread * mean, axis=0, keepdims=True)
    gram = lax.dot_general(
        spread, spread, (((0,), (0,)), ((), ())),
        precision=HIGHEST, preferred_element_type=jnp.float32,
    )
    rows = lax.broadcasted_iota(jnp.int32, (ens, ens), 0)
    lanes = lax.broadcasted_iota(jnp.int32, (ens, ens), 1)
    square[...] = jnp.where(rows == lanes, 1.0, 0.0) + gram
    inverse_factor(square)
    inverse = square[...]
    shift = jnp.sum(inverse * project, axis=1, keepdims=True)
    shift = jnp.sum(inverse * shift, axis=0, keepdims=True)
    combined = inverse + shift * root
    level = (1.0 - jnp.sum(combined, axis=1, keepdims=True)) * (1.0 / ens)
    combined = combined + level
    shift_column = jnp.sum(jnp.where(rows == lanes, shift, 0.0), axis=1, keepdims=True) * root
    square[...] = jnp.broadcast_to(shift_column, (ens, width))
    own_rows = pl.ds(pl.multiple_of(half * members, 8), members)

    @pl.when(half > 0)
    def _():
        own_shift = square[own_rows, :]
        sub = lax.broadcasted_iota(jnp.int32, (8, width), 0)

        def add_up(z, carry):
            for field in range(3):
                state = own[field, z]
                plain = jnp.sum(state, axis=0, keepdims=True)
                shifted = jnp.sum(state * own_shift, axis=0, keepdims=True)
                sums[field, z] = jnp.where(sub == 0, plain, jnp.where(sub == 1, shifted, 0.0))
            return carry

        lax.fori_loop(0, depth, add_up, 0)

    sum_copies = [
        pltpu.make_async_remote_copy(
            src_ref=sums,
            dst_ref=other.at[hop - 1, :, :, pl.ds(0, 8), :],
            send_sem=sum_send.at[hop - 1],
            recv_sem=sum_recv.at[hop - 1],
            device_id=(slab, lax.rem(half + hop, halves)),
            device_id_type=MESH,
        )
        for hop in range(1, halves)
    ]
    for hop, copy in enumerate(sum_copies, 1):
        pl.when(half + hop >= halves)(copy.start)

    combined = pltpu.roll(combined, lax.rem(ens - half * members, ens), 1)
    ahead = lanes // members
    at = lanes - ahead * members
    of_sums = jnp.where(at == 0, level, jnp.where(at == 1, 1.0, 0.0))
    square[...] = jnp.where((ahead > 0) & (half + ahead < halves), of_sums, combined)
    for hop, copy in enumerate(sum_copies, 1):
        pl.when(half < hop)(copy.wait_recv)
    weight_high, weight_low = split(square[own_rows, :])
    weights = jnp.concatenate([weight_high, weight_high, weight_low], axis=1)

    for field, start, count, copies in pieces:
        for hop, copy in enumerate(copies, 1):
            pl.when(half >= hop)(copy.wait_recv)
        for z in range(start, start + count, 2):
            parts = []
            for d in (z, z + 1):
                blocks = [own[field, d]] + [
                    other[halves - q - 1, field, d] for q in range(1, halves)
                ]
                parts.append(jnp.concatenate(blocks, axis=0))
            state_high, state_low = split(jnp.concatenate(parts, axis=1))
            mixed = jnp.dot(
                weights,
                jnp.concatenate([state_high, state_low, state_high], axis=0),
                preferred_element_type=jnp.float32,
            )
            for i, d in enumerate((z, z + 1)):
                block = mixed[:, i * width : (i + 1) * width]
                if field == SPEED:
                    out_v_ref[pl.ds(d, members, stride=depth), :] = block
                else:
                    out_hc_ref[pl.ds(field * depth + d, members, stride=2 * depth), :] = block

    for _, _, _, copies in pieces:
        for hop, copy in enumerate(copies, 1):
            pl.when(half + hop < halves)(copy.wait_send)
    for hop, copy in enumerate(sum_copies, 1):
        pl.when(half + hop >= halves)(copy.wait_send)
    pltpu.make_async_copy(rest, rest, seen_send.at[0]).wait()

    @pl.when(jnp.logical_not(first))
    def _():
        for copy in up:
            copy.wait_send()

    @pl.when(jnp.logical_not(last))
    def _():
        for copy in down:
            copy.wait_send()


def on_device(slabs, halves, member_heat_solute, velocity, phase_mask, obs_index, obs_value, obs_error):
    members, _, depth, width = member_heat_solute.shape
    ens = members * halves
    held = pl.BlockSpec(memory_space=pltpu.VMEM)
    anywhere = pl.BlockSpec(memory_space=pltpu.HBM)
    hc, vel = pl.pallas_call(
        functools.partial(kernel, slabs, halves),
        out_shape=(
            pltpu.VMEM((members * 2 * depth, width), jnp.float32),
            pltpu.VMEM((members * depth, width), jnp.float32),
        ),
        in_specs=[anywhere] * 6,
        out_specs=(held, held),
        scratch_shapes=[
            pltpu.VMEM((depth, width), jnp.int32),
            pltpu.SMEM(obs_index.shape, jnp.int32),
            pltpu.SMEM(obs_value.shape, jnp.float32),
            pltpu.SMEM(obs_error.shape, jnp.float32),
            pltpu.VMEM((members * 2 * depth, width), jnp.float32),
            pltpu.VMEM((members * depth, width), jnp.float32),
            pltpu.VMEM((3, depth + 4, members, width), jnp.float32),
            pltpu.VMEM((depth + 4, 8, width), jnp.float32),
            pltpu.VMEM((3, depth, members, width), jnp.float32),
            pltpu.VMEM((halves - 1, 3, depth, members, width), jnp.float32),
            pltpu.VMEM((3, depth, 8, width), jnp.float32),
            pltpu.VMEM((slabs * halves, 8, ens), jnp.float32),
            pltpu.VMEM((ens, ens), jnp.float32),
            pltpu.SemaphoreType.DMA((6,)),
            pltpu.SemaphoreType.DMA((2, 2)),
            pltpu.SemaphoreType.DMA((2, 2)),
            pltpu.SemaphoreType.DMA((halves - 1, 3 * depth // 2)),
            pltpu.SemaphoreType.DMA((halves - 1, 3 * depth // 2)),
            pltpu.SemaphoreType.DMA((1,)),
            pltpu.SemaphoreType.DMA((1,)),
            pltpu.SemaphoreType.DMA((halves - 1,)),
            pltpu.SemaphoreType.DMA((halves - 1,)),
        ],
        compiler_params=pltpu.CompilerParams(
            collective_id=0, has_side_effects=True, vmem_limit_bytes=40 * 1024 * 1024
        ),
    )(
        *[
            pltpu.with_memory_space_constraint(x, pltpu.HBM)
            for x in (
                member_heat_solute.reshape(-1, width),
                velocity.reshape(-1, width),
                phase_mask,
                obs_index,
                obs_value,
                obs_error,
            )
        ]
    )
    return hc.reshape(members, 2, depth, width), vel.reshape(members, depth, width)


def solution(mesh):
    return jax.shard_map(
        functools.partial(on_device, mesh.shape["space"], mesh.shape["mem"]),
        mesh=mesh,
        in_specs=(
            P("mem", None, "space", None),
            P("mem", "space", None),
            P("space", None),
            P("space"),
            P("space"),
            P("space"),
        ),
        out_specs=(P("mem", None, "space", None), P("mem", "space", None)),
        check_vma=False,
    )
```

profile of v0, /device:TPU:0, one launch (start us, length us, event | category | flops | bytes accessed | tf_op | source)
XLA Modules:
  0.0 45.7 jit_solution(3152112889261508505)
XLA Ops:
  0.6 43.3 %shard_map.77 = (f32[2048,128]{1,0:T(8,128)S(1)}, f32[1024,128]{1,0:T(8,128)S(1)}) custom-call(f32[2048,128]{1,0:T(8,128)} %bitcast.6, f32[1024,128]{1,0:T(8,128)} %bitcast.7, s32[16,128]{1,0:T(8,128)} %phase_ref.1, s32[16]{0:T(128)} %cell_ref.1, f32[16]{0:T(128)} %datum_ref.1, f32[16]{0:T(128)} %deviate_ref.1), custom_call_target="tpu_custom_call" | custom-call | tf_op jit(solution)/shard_map/pallas_call | solution.py:473
  43.9 1.0 %copy.10 = f32[64,2,16,128]{3,2,1,0:T(8,128)} copy(f32[64,2,16,128]{3,2,1,0:T(8,128)S(1)} %bitcast.4) | data formatting | bytes 2097152
  44.9 0.8 %copy.11 = f32[64,16,128]{2,1,0:T(8,128)} copy(f32[64,16,128]{2,1,0:T(8,128)S(1)} %bitcast.5) | data formatting | bytes 1048576
where the time goes:
time: 45.9 us; the launch traced here: 45.7 us
  Pallas kernels  43.3 us (94%)
  local copies, waits for them, and re-layouts  1.77 us (4%)
  between operations  0.64 us (1%)
    pallas_call x1, Pallas kernels, on_device(): pl.pallas_call(functools.partial(kernel, slabs, halves), out_shape=(pltpu...  43.3 us
    unnamed x2, local copies, waits for them, and re-layouts  1.77 us

commit v1 on v0

--- a/solution.py
+++ b/solution.py
@@ -122,18 +122,16 @@
     slabs, halves,
     hc_ref, v_ref, phase_ref, cell_ref, datum_ref, deviate_ref,
     out_hc_ref, out_v_ref,
-    mask_ref, index_ref, value_ref, error_ref, hc, vel, raw, mushy, own, other, sums, seen, square,
-    in_sem, halo_send, halo_recv, state_send, state_recv, seen_send, seen_recv, sum_send, sum_recv,
+    mask_ref, index_ref, value_ref, error_ref, hc, vel, raw, mushy, own, other, sums, sums_in, part, seen, square,
+    in_sem, halo_send, halo_recv, state_send, state_recv, part_send, part_recv, seen_send, seen_recv, sum_send, sum_recv,
 ):
     members = own.shape[2]
     width = own.shape[3]
     depth = own.shape[1]
     groups = members // 8
-    everyone = slabs * halves
     ens = members * halves
     slab = lax.axis_index("space")
     half = lax.axis_index("mem")
-    me = slab * halves + half
     first = slab == 0
     last = slab == slabs - 1
 
@@ -154,13 +152,16 @@
     barrier = pltpu.get_barrier_semaphore()
 
     def greet(step, carry):
-        peer = lax.rem(me + step, everyone)
         pl.semaphore_signal(
-            barrier, inc=1, device_id=(peer // halves, lax.rem(peer, halves)), device_id_type=MESH
+            barrier, inc=1, device_id=(lax.rem(slab + step, slabs), half), device_id_type=MESH
         )
         return carry
 
-    lax.fori_loop(1, everyone, greet, 0)
+    for hop in range(1, halves):
+        pl.semaphore_signal(
+            barrier, inc=1, device_id=(slab, lax.rem(half + hop, halves)), device_id_type=MESH
+        )
+    lax.fori_loop(1, slabs, greet, 0)
 
     load_mask.wait()
     for z in range(depth):
@@ -215,7 +216,7 @@
         raw[:, depth + 2 : depth + 4] = jnp.zeros((3, 2, members, width), jnp.float32)
         mushy[depth + 2 : depth + 4] = jnp.zeros((2, 8, width), jnp.float32)
 
-    pl.semaphore_wait(barrier, everyone - 1)
+    pl.semaphore_wait(barrier, slabs + halves - 2)
 
     @pl.when(jnp.logical_not(first))
     def _():
@@ -318,23 +319,20 @@
     square[...] = jnp.zeros((ens, width), jnp.float32)
     square[pl.ds(pl.multiple_of(half * members, 8), members), :] = (observed - value) / error
     turned = square[...].T
-    seen[me] = turned[0:8] + pltpu.roll(turned[8:16], ens // 2, 1)
-
-    def tell_copy(peer):
-        return pltpu.make_async_remote_copy(
-            src_ref=seen.at[me],
-            dst_ref=seen.at[me],
-            send_sem=seen_send.at[0],
-            recv_sem=seen_recv.at[0],
-            device_id=(peer // halves, lax.rem(peer, halves)),
+    part[half] = turned[0:8] + pltpu.roll(turned[8:16], ens // 2, 1)
+    part_copies = [
+        pltpu.make_async_remote_copy(
+            src_ref=part.at[half],
+            dst_ref=part.at[half],
+            send_sem=part_send.at[hop - 1],
+            recv_sem=part_recv.at[0],
+            device_id=(slab, lax.rem(half + hop, halves)),
             device_id_type=MESH,
         )
-
-    def tell(step, carry):
-        tell_copy(lax.rem(me + step, everyone)).start()
-        return carry
-
-    lax.fori_loop(1, everyone, tell, 0)
+        for hop in range(1, halves)
+    ]
+    for copy in part_copies:
+        copy.start()
 
     for z in (0, depth - 2):
         send(SPEED, z, 2)
@@ -349,20 +347,41 @@
         def _():
             other[hop - 1, :, :, 8:, :] = jnp.zeros((3, depth, members - 8, width), jnp.float32)
 
-    rest = seen.at[pl.ds(0, everyone - 1)]
-    pltpu.make_async_copy(rest, rest, seen_recv.at[0]).wait()
-
-    got = seen[...].reshape(slabs, halves, 8, ens)
-    place = lax.broadcasted_iota(jnp.int32, (slabs, 8, ens), 2)
-    low = jnp.zeros((slabs, 8, ens), jnp.float32)
-    high = jnp.zeros((slabs, 8, ens), jnp.float32)
+    others = part.at[pl.ds(0, halves - 1)]
+    pltpu.make_async_copy(others, others, part_recv.at[0]).wait()
+    place = lax.broadcasted_iota(jnp.int32, (8, ens), 1)
+    low = jnp.zeros((8, ens), jnp.float32)
+    high = jnp.zeros((8, ens), jnp.float32)
     for m in range(halves):
         mine = (place >= m * members) & (place < (m + 1) * members)
-        low = jnp.where(mine, got[:, m], low)
-        high = jnp.where(mine, pltpu.roll(got[:, m], ens // 2, 2), high)
-    deviation = jnp.concatenate(
-        [low.reshape(slabs * 8, ens), high.reshape(slabs * 8, ens)], axis=0
-    )
+        low = jnp.where(mine, part[m], low)
+        high = jnp.where(mine, pltpu.roll(part[m], ens // 2, 1), high)
+    seen[slab, 0:8] = low
+    seen[slab, 8:16] = high
+
+    def tell(step, carry):
+        pltpu.make_async_remote_copy(
+            src_ref=seen.at[slab],
+            dst_ref=seen.at[slab],
+            send_sem=seen_send.at[0],
+            recv_sem=seen_recv.at[0],
+            device_id=(lax.rem(slab + step, slabs), half),
+            device_id_type=MESH,
+        ).start()
+        return carry
+
+    lax.fori_loop(1, slabs, tell, 0)
+
+    for hop in range(1, halves):
+
+        @pl.when(half < hop)
+        def _():
+            other[hop - 1, :, :, 8:, :] = jnp.zeros((3, depth, members - 8, width), jnp.float32)
+
+    rest = seen.at[pl.ds(0, slabs - 1)]
+    pltpu.make_async_copy(rest, rest, seen_recv.at[0]).wait()
+
+    deviation = seen[...].reshape(slabs * 16, ens)
     mean = jnp.sum(deviation, axis=1, keepdims=True) * (1.0 / ens)
     root = 1.0 / (ens - 1.0) ** 0.5
     spread = (deviation - mean) * root
@@ -388,22 +407,16 @@
     @pl.when(half > 0)
     def _():
         own_shift = square[own_rows, :]
-        sub = lax.broadcasted_iota(jnp.int32, (8, width), 0)
-
-        def add_up(z, carry):
+        for z in range(depth):
             for field in range(3):
                 state = own[field, z]
-                plain = jnp.sum(state, axis=0, keepdims=True)
-                shifted = jnp.sum(state * own_shift, axis=0, keepdims=True)
-                sums[field, z] = jnp.where(sub == 0, plain, jnp.where(sub == 1, shifted, 0.0))
-            return carry
-
-        lax.fori_loop(0, depth, add_up, 0)
+                sums[field, 0, z : z + 1, :] = jnp.sum(state, axis=0, keepdims=True)
+                sums[field, 1, z : z + 1, :] = jnp.sum(state * own_shift, axis=0, keepdims=True)
 
     sum_copies = [
         pltpu.make_async_remote_copy(
             src_ref=sums,
-            dst_ref=other.at[hop - 1, :, :, pl.ds(0, 8), :],
+            dst_ref=sums_in.at[hop - 1],
             send_sem=sum_send.at[hop - 1],
             recv_sem=sum_recv.at[hop - 1],
             device_id=(slab, lax.rem(half + hop, halves)),
@@ -420,7 +433,19 @@
     of_sums = jnp.where(at == 0, level, jnp.where(at == 1, 1.0, 0.0))
     square[...] = jnp.where((ahead > 0) & (half + ahead < halves), of_sums, combined)
     for hop, copy in enumerate(sum_copies, 1):
-        pl.when(half < hop)(copy.wait_recv)
+
+        @pl.when(half < hop)
+        def _():
+            copy.wait_recv()
+            sub = lax.broadcasted_iota(jnp.int32, (8, width), 0)
+            for field in range(3):
+                for z in range(depth):
+                    plain = sums_in[hop - 1, field, 0, z : z + 1, :]
+                    shifted = sums_in[hop - 1, field, 1, z : z + 1, :]
+                    other[hop - 1, field, z, 0:8, :] = jnp.where(
+                        sub == 0, plain, jnp.where(sub == 1, shifted, 0.0)
+                    )
+
     weight_high, weight_low = split(square[own_rows, :])
     weights = jnp.concatenate([weight_high, weight_high, weight_low], axis=1)
 
@@ -452,6 +477,8 @@
             pl.when(half + hop < halves)(copy.wait_send)
     for hop, copy in enumerate(sum_copies, 1):
         pl.when(half + hop >= halves)(copy.wait_send)
+    for copy in part_copies:
+        copy.wait_send()
     pltpu.make_async_copy(rest, rest, seen_send.at[0]).wait()
 
     @pl.when(jnp.logical_not(first))
@@ -463,6 +490,17 @@
     def _():
         for copy in down:
             copy.wait_send()
+
+
+def write_back(hc, vel, out_hc, out_vel, sem):
+    copies = [
+        pltpu.make_async_copy(hc, out_hc, sem.at[0]),
+        pltpu.make_async_copy(vel, out_vel, sem.at[1]),
+    ]
+    for copy in copies:
+        copy.start()
+    for copy in copies:
+        copy.wait()
 
 
 def on_device(slabs, halves, member_heat_solute, velocity, phase_mask, obs_index, obs_value, obs_error):
@@ -489,14 +527,18 @@
             pltpu.VMEM((depth + 4, 8, width), jnp.float32),
             pltpu.VMEM((3, depth, members, width), jnp.float32),
             pltpu.VMEM((halves - 1, 3, depth, members, width), jnp.float32),
-            pltpu.VMEM((3, depth, 8, width), jnp.float32),
-            pltpu.VMEM((slabs * halves, 8, ens), jnp.float32),
+            pltpu.VMEM((3, 2, depth, width), jnp.float32),
+            pltpu.VMEM((halves - 1, 3, 2, depth, width), jnp.float32),
+            pltpu.VMEM((halves, 8, ens), jnp.float32),
+            pltpu.VMEM((slabs, 16, ens), jnp.float32),
             pltpu.VMEM((ens, ens), jnp.float32),
             pltpu.SemaphoreType.DMA((6,)),
             pltpu.SemaphoreType.DMA((2, 2)),
             pltpu.SemaphoreType.DMA((2, 2)),
             pltpu.SemaphoreType.DMA((halves - 1, 3 * depth // 2)),
             pltpu.SemaphoreType.DMA((halves - 1, 3 * depth // 2)),
+            pltpu.SemaphoreType.DMA((halves - 1,)),
+            pltpu.SemaphoreType.DMA((1,)),
             pltpu.SemaphoreType.DMA((1,)),
             pltpu.SemaphoreType.DMA((1,)),
             pltpu.SemaphoreType.DMA((halves - 1,)),
@@ -518,6 +560,20 @@
             )
         ]
     )
+    hc, vel = pl.pallas_call(
+        write_back,
+        out_shape=(
+            jax.ShapeDtypeStruct(hc.shape, jnp.float32),
+            jax.ShapeDtypeStruct(vel.shape, jnp.float32),
+        ),
+        in_specs=[held, held],
+        out_specs=(anywhere, anywhere),
+        scratch_shapes=[pltpu.SemaphoreType.DMA((2,))],
+        compiler_params=pltpu.CompilerParams(vmem_limit_bytes=16 * 1024 * 1024),
+    )(
+        pltpu.with_memory_space_constraint(hc, pltpu.VMEM),
+        pltpu.with_memory_space_constraint(vel, pltpu.VMEM),
+    )
     return hc.reshape(members, 2, depth, width), vel.reshape(members, depth, width)
 
 

time: 45.9 us -> 43 us (0.937)
  local copies, waits for them, and re-layouts: 1.77 us -> 0 us
  Pallas kernels: 43.3 us -> 42.2 us
    pallas_call x1, Pallas kernels: 43.3 us -> 41 us  [on_device(): pl.pallas_call(functools.partial(kernel, slabs, halves), out_shape=(pltpu...]
    unnamed x2 -> x0, local copies, waits for them, and re-layouts: 1.77 us -> none
    pallas_call x0 -> x1, Pallas kernels: none -> 1.16 us  [on_device(): pl.pallas_call(write_back, out_shape=(jax.ShapeDtypeStruct(hc.shape, jnp....]
where the time goes in v1:
time: 43 us; the launch traced here: 42.8 us
  Pallas kernels  42.2 us (98%)
  between operations  0.64 us (1%)
    pallas_call x1, Pallas kernels, on_device(): pl.pallas_call(functools.partial(kernel, slabs, halves), out_shape=(pltpu...  41 us
    pallas_call x1, Pallas kernels, on_device(): pl.pallas_call(write_back, out_shape=(jax.ShapeDtypeStruct(hc.shape, jnp....  1.16 us

profile of v1, /device:TPU:0, one launch (start us, length us, event | category | flops | bytes accessed | tf_op | source)
XLA Modules:
  0.0 42.8 jit_solution(5093029381017130239)
XLA Ops:
  0.6 41.0 %shard_map.77 = (f32[2048,128]{1,0:T(8,128)S(1)}, f32[1024,128]{1,0:T(8,128)S(1)}) custom-call(f32[2048,128]{1,0:T(8,128)} %bitcast.4, f32[1024,128]{1,0:T(8,128)} %bitcast.5, s32[16,128]{1,0:T(8,128)} %phase_ref.1, s32[16]{0:T(128)} %cell_ref.1, f32[16]{0:T(128)} %datum_ref.1, f32[16]{0:T(128)} %deviate_ref.1), custom_call_target="tpu_custom_call" | custom-call | tf_op jit(solution)/shard_map/pallas_call | solution.py:511
  41.7 1.2 %shard_map.78 = (f32[2048,128]{1,0:T(8,128)}, f32[1024,128]{1,0:T(8,128)}) custom-call(f32[2048,128]{1,0:T(8,128)S(1)} %get-tuple-element.6.hc, f32[1024,128]{1,0:T(8,128)S(1)} %get-tuple-element.7.vel), custom_call_target="tpu_custom_call" | custom-call | tf_op jit(solution)/shard_map/pallas_call | solution.py:563

commit v2 on v1

--- a/solution.py
+++ b/solution.py
@@ -188,46 +188,6 @@
         return carry
 
     lax.fori_loop(0, groups, inner_speed, 0)
-    load_hc.wait()
-    relayout_pair((0, 1, depth - 2, depth - 1))
-
-    def halo(direction, source, target, to, part):
-        ref = raw if part == 0 else mushy
-        pick = (lambda r, a: r.at[:, pl.ds(a, 2)]) if part == 0 else (lambda r, a: r.at[pl.ds(a, 2)])
-        return pltpu.make_async_remote_copy(
-            src_ref=pick(ref, source),
-            dst_ref=pick(ref, target),
-            send_sem=halo_send.at[direction, part],
-            recv_sem=halo_recv.at[direction, part],
-            device_id=(to, half),
-            device_id_type=MESH,
-        )
-
-    up = [halo(0, 2, depth + 2, lax.rem(slab + slabs - 1, slabs), part) for part in range(2)]
-    down = [halo(1, depth, 0, lax.rem(slab + 1, slabs), part) for part in range(2)]
-
-    @pl.when(first)
-    def _():
-        raw[:, 0:2] = jnp.zeros((3, 2, members, width), jnp.float32)
-        mushy[0:2] = jnp.zeros((2, 8, width), jnp.float32)
-
-    @pl.when(last)
-    def _():
-        raw[:, depth + 2 : depth + 4] = jnp.zeros((3, 2, members, width), jnp.float32)
-        mushy[depth + 2 : depth + 4] = jnp.zeros((2, 8, width), jnp.float32)
-
-    pl.semaphore_wait(barrier, slabs + halves - 2)
-
-    @pl.when(jnp.logical_not(first))
-    def _():
-        for copy in up:
-            copy.start()
-
-    @pl.when(jnp.logical_not(last))
-    def _():
-        for copy in down:
-            copy.start()
-
     pieces = []
 
     def send(field, start, count):
@@ -249,8 +209,47 @@
         pieces.append((field, start, count, copies))
 
     middle = depth // 2
-    for z in range(2, depth - 2, 2):
-        send(SPEED, z, 2)
+    pl.semaphore_wait(barrier, slabs + halves - 2)
+    send(SPEED, 2, depth - 4)
+    load_hc.wait()
+    relayout_pair((0, 1, depth - 2, depth - 1))
+
+    def halo(direction, source, target, to, part):
+        ref = raw if part == 0 else mushy
+        pick = (lambda r, a: r.at[:, pl.ds(a, 2)]) if part == 0 else (lambda r, a: r.at[pl.ds(a, 2)])
+        return pltpu.make_async_remote_copy(
+            src_ref=pick(ref, source),
+            dst_ref=pick(ref, target),
+            send_sem=halo_send.at[direction, part],
+            recv_sem=halo_recv.at[direction, part],
+            device_id=(to, half),
+            device_id_type=MESH,
+        )
+
+    up = [halo(0, 2, depth + 2, lax.rem(slab + slabs - 1, slabs), part) for part in range(2)]
+    down = [halo(1, depth, 0, lax.rem(slab + 1, slabs), part) for part in range(2)]
+
+    @pl.when(first)
+    def _():
+        raw[:, 0:2] = jnp.zeros((3, 2, members, width), jnp.float32)
+        mushy[0:2] = jnp.zeros((2, 8, width), jnp.float32)
+
+    @pl.when(last)
+    def _():
+        raw[:, depth + 2 : depth + 4] = jnp.zeros((3, 2, members, width), jnp.float32)
+        mushy[depth + 2 : depth + 4] = jnp.zeros((2, 8, width), jnp.float32)
+
+    @pl.when(jnp.logical_not(first))
+    def _():
+        for copy in up:
+            copy.start()
+
+    @pl.when(jnp.logical_not(last))
+    def _():
+        for copy in down:
+            copy.start()
+
+    middle = depth // 2
     relayout_pair(range(2, depth - 2))
 
     def inner_pair(group, carry):
@@ -266,8 +265,7 @@
         return carry
 
     lax.fori_loop(0, groups, inner_pair, 0)
-    for z in range(2, middle, 2):
-        send(HEAT, z, 2)
+    send(HEAT, 2, middle - 2)
 
     @pl.when(jnp.logical_not(last))
     def _():
@@ -334,18 +332,14 @@
     for copy in part_copies:
         copy.start()
 
-    for z in (0, depth - 2):
-        send(SPEED, z, 2)
-    for z in (0, *range(middle, depth, 2)):
-        send(HEAT, z, 2)
-    for z in range(0, depth, 2):
-        send(SOLUTE, z, 2)
-
-    for hop in range(1, halves):
-
-        @pl.when(half < hop)
-        def _():
-            other[hop - 1, :, :, 8:, :] = jnp.zeros((3, depth, members - 8, width), jnp.float32)
+    send(SPEED, 0, 2)
+    send(SPEED, depth - 2, 2)
+    send(HEAT, 0, 2)
+    send(HEAT, middle, middle)
+    send(SOLUTE, 0, middle)
+    send(SOLUTE, middle, middle - 4)
+    send(SOLUTE, depth - 4, 2)
+    send(SOLUTE, depth - 2, 2)
 
     others = part.at[pl.ds(0, halves - 1)]
     pltpu.make_async_copy(others, others, part_recv.at[0]).wait()
@@ -432,6 +426,35 @@
     at = lanes - ahead * members
     of_sums = jnp.where(at == 0, level, jnp.where(at == 1, 1.0, 0.0))
     square[...] = jnp.where((ahead > 0) & (half + ahead < halves), of_sums, combined)
+    weights = square[own_rows, :]
+
+    def stack(part):
+        part_high, part_low = split(part)
+        return jnp.concatenate([part_high, part_high, part_low], axis=1)
+
+    own_weights = stack(weights[:, :members])
+    other_weights = stack(weights[:, members:])
+
+    def mix(field, z, blocks, chosen, add):
+        parts = [jnp.concatenate(blocks(d), axis=0) for d in (z, z + 1)]
+        state_high, state_low = split(jnp.concatenate(parts, axis=1))
+        mixed = jnp.dot(
+            chosen,
+            jnp.concatenate([state_high, state_low, state_high], axis=0),
+            preferred_element_type=jnp.float32,
+        )
+        for i, d in enumerate((z, z + 1)):
+            block = mixed[:, i * width : (i + 1) * width]
+            if field == SPEED:
+                out, at = out_v_ref, pl.ds(d, members, stride=depth)
+            else:
+                out, at = out_hc_ref, pl.ds(field * depth + d, members, stride=2 * depth)
+            out[at, :] = out[at, :] + block if add else block
+
+    for field in range(3):
+        for z in range(0, depth, 2):
+            mix(field, z, lambda d: [own[field, d]], own_weights, False)
+
     for hop, copy in enumerate(sum_copies, 1):
 
         @pl.when(half < hop)
@@ -446,31 +469,17 @@
                         sub == 0, plain, jnp.where(sub == 1, shifted, 0.0)
                     )
 
-    weight_high, weight_low = split(square[own_rows, :])
-    weights = jnp.concatenate([weight_high, weight_high, weight_low], axis=1)
-
     for field, start, count, copies in pieces:
         for hop, copy in enumerate(copies, 1):
             pl.when(half >= hop)(copy.wait_recv)
         for z in range(start, start + count, 2):
-            parts = []
-            for d in (z, z + 1):
-                blocks = [own[field, d]] + [
-                    other[halves - q - 1, field, d] for q in range(1, halves)
-                ]
-                parts.append(jnp.concatenate(blocks, axis=0))
-            state_high, state_low = split(jnp.concatenate(parts, axis=1))
-            mixed = jnp.dot(
-                weights,
-                jnp.concatenate([state_high, state_low, state_high], axis=0),
-                preferred_element_type=jnp.float32,
+            mix(
+                field,
+                z,
+                lambda d: [other[halves - q - 1, field, d] for q in range(1, halves)],
+                other_weights,
+                True,
             )
-            for i, d in enumerate((z, z + 1)):
-                block = mixed[:, i * width : (i + 1) * width]
-                if field == SPEED:
-                    out_v_ref[pl.ds(d, members, stride=depth), :] = block
-                else:
-                    out_hc_ref[pl.ds(field * depth + d, members, stride=2 * depth), :] = block
 
     for _, _, _, copies in pieces:
         for hop, copy in enumerate(copies, 1):
@@ -493,10 +502,14 @@
 
 
 def write_back(hc, vel, out_hc, out_vel, sem):
-    copies = [
-        pltpu.make_async_copy(hc, out_hc, sem.at[0]),
-        pltpu.make_async_copy(vel, out_vel, sem.at[1]),
-    ]
+    copies = []
+    for source, target, count in ((hc, out_hc, 4), (vel, out_vel, 2)):
+        rows = source.shape[0] // count
+        for i in range(count):
+            at = pl.ds(i * rows, rows)
+            copies.append(
+                pltpu.make_async_copy(source.at[at], target.at[at], sem.at[len(copies)])
+            )
     for copy in copies:
         copy.start()
     for copy in copies:
@@ -535,8 +548,8 @@
             pltpu.SemaphoreType.DMA((6,)),
             pltpu.SemaphoreType.DMA((2, 2)),
             pltpu.SemaphoreType.DMA((2, 2)),
-            pltpu.SemaphoreType.DMA((halves - 1, 3 * depth // 2)),
-            pltpu.SemaphoreType.DMA((halves - 1, 3 * depth // 2)),
+            pltpu.SemaphoreType.DMA((halves - 1, 10)),
+            pltpu.SemaphoreType.DMA((halves - 1, 10)),
             pltpu.SemaphoreType.DMA((halves - 1,)),
             pltpu.SemaphoreType.DMA((1,)),
             pltpu.SemaphoreType.DMA((1,)),
@@ -568,7 +581,7 @@
         ),
         in_specs=[held, held],
         out_specs=(anywhere, anywhere),
-        scratch_shapes=[pltpu.SemaphoreType.DMA((2,))],
+        scratch_shapes=[pltpu.SemaphoreType.DMA((6,))],
         compiler_params=pltpu.CompilerParams(vmem_limit_bytes=16 * 1024 * 1024),
     )(
         pltpu.with_memory_space_constraint(hc, pltpu.VMEM),

time: 43 us -> 42.8 us (level)
  no operation moved by 1% of the time
where the time goes in v2:
time: 42.8 us; the launch traced here: 42.6 us
  Pallas kernels  42 us (98%)
  between operations  0.64 us (1%)
    pallas_call x1, Pallas kernels, on_device(): pl.pallas_call(functools.partial(kernel, slabs, halves), out_shape=(pltpu...  40.8 us
    pallas_call x1, Pallas kernels, on_device(): pl.pallas_call(write_back, out_shape=(jax.ShapeDtypeStruct(hc.shape, jnp....  1.19 us

profile of v2, /device:TPU:0, one launch (start us, length us, event | category | flops | bytes accessed | tf_op | source)
XLA Modules:
  0.0 42.6 jit_solution(8554552363743570492)
XLA Ops:
  0.6 40.8 %shard_map.77 = (f32[2048,128]{1,0:T(8,128)S(1)}, f32[1024,128]{1,0:T(8,128)S(1)}) custom-call(f32[2048,128]{1,0:T(8,128)} %bitcast.4, f32[1024,128]{1,0:T(8,128)} %bitcast.5, s32[16,128]{1,0:T(8,128)} %phase_ref.1, s32[16]{0:T(128)} %cell_ref.1, f32[16]{0:T(128)} %datum_ref.1, f32[16]{0:T(128)} %deviate_ref.1), custom_call_target="tpu_custom_call" | custom-call | tf_op jit(solution)/shard_map/pallas_call | solution.py:524
  41.4 1.2 %shard_map.78 = (f32[2048,128]{1,0:T(8,128)}, f32[1024,128]{1,0:T(8,128)}) custom-call(f32[2048,128]{1,0:T(8,128)S(1)} %get-tuple-element.6.hc, f32[1024,128]{1,0:T(8,128)S(1)} %get-tuple-element.7.vel), custom_call_target="tpu_custom_call" | custom-call | tf_op jit(solution)/shard_map/pallas_call | solution.py:576

commit v3 on v2

--- a/solution.py
+++ b/solution.py
@@ -143,34 +143,36 @@
         pltpu.make_async_copy(datum_ref, value_ref, in_sem.at[4]),
         pltpu.make_async_copy(deviate_ref, error_ref, in_sem.at[5]),
     ]
+    load_v.start()
     load_mask.start()
-    load_v.start()
+
+    barrier = pltpu.get_barrier_semaphore()
+
+    def greet(step, carry):
+        pl.semaphore_signal(
+            barrier, inc=1, device_id=(lax.rem(slab + step, slabs), half), device_id_type=MESH
+        )
+        return carry
+
+    for hop in range(1, halves):
+        pl.semaphore_signal(
+            barrier, inc=1, device_id=(slab, lax.rem(half + hop, halves)), device_id_type=MESH
+        )
+    lax.fori_loop(1, slabs, greet, 0)
     load_hc.start()
     for load in load_observed:
         load.start()
-
-    barrier = pltpu.get_barrier_semaphore()
-
-    def greet(step, carry):
-        pl.semaphore_signal(
-            barrier, inc=1, device_id=(lax.rem(slab + step, slabs), half), device_id_type=MESH
-        )
-        return carry
-
-    for hop in range(1, halves):
-        pl.semaphore_signal(
-            barrier, inc=1, device_id=(slab, lax.rem(half + hop, halves)), device_id_type=MESH
-        )
-    lax.fori_loop(1, slabs, greet, 0)
 
     load_mask.wait()
     for z in range(depth):
         row = mask_ref[z : z + 1, :].astype(jnp.float32)
         mushy[z + 2] = jnp.broadcast_to(row, (8, width))
 
-    def relayout_speed(zs):
-        for z in zs:
-            raw[SPEED, z + 2] = vel[pl.ds(z, members, stride=depth), :]
+    def relayout_speed(start, count):
+        for z in range(depth):
+            raw[SPEED, z + 2, start : start + count, :] = vel[
+                pl.ds(start * depth + z, count, stride=depth), :
+            ]
 
     def relayout_pair(zs):
         for z in zs:
@@ -178,7 +180,6 @@
             raw[SOLUTE, z + 2] = hc[pl.ds(depth + z, members, stride=2 * depth), :]
 
     load_v.wait()
-    relayout_speed(range(depth))
 
     def inner_speed(group, carry):
         at = pl.ds(pl.multiple_of(group * 8, 8), 8)
@@ -187,17 +188,18 @@
         own[SPEED, 2 : depth - 2, at, :] = advance_speed(speed, mask[1:-1])
         return carry
 
-    lax.fori_loop(0, groups, inner_speed, 0)
     pieces = []
 
-    def send(field, start, count):
+    def send(field, start, count, first_member=0, some=members, mixed=True):
         number = len(pieces)
         copies = []
         for hop in range(1, halves):
             copies.append(
                 pltpu.make_async_remote_copy(
-                    src_ref=own.at[field, pl.ds(start, count)],
-                    dst_ref=other.at[hop - 1, field, pl.ds(start, count)],
+                    src_ref=own.at[field, pl.ds(start, count), pl.ds(first_member, some)],
+                    dst_ref=other.at[
+                        hop - 1, field, pl.ds(start, count), pl.ds(first_member, some)
+                    ],
                     send_sem=state_send.at[hop - 1, number],
                     recv_sem=state_recv.at[hop - 1, number],
                     device_id=(slab, lax.rem(half + hop, halves)),
@@ -206,11 +208,17 @@
             )
         for hop, copy in enumerate(copies, 1):
             pl.when(half + hop < halves)(copy.start)
-        pieces.append((field, start, count, copies))
+        pieces.append((field, start, count if mixed else 0, copies))
 
     middle = depth // 2
+    some = members // 2
+    relayout_speed(0, some)
+    lax.fori_loop(0, groups // 2, inner_speed, 0)
     pl.semaphore_wait(barrier, slabs + halves - 2)
-    send(SPEED, 2, depth - 4)
+    send(SPEED, 2, depth - 4, 0, some, mixed=False)
+    relayout_speed(some, some)
+    lax.fori_loop(groups // 2, groups, inner_speed, 0)
+    send(SPEED, 2, depth - 4, some, some)
     load_hc.wait()
     relayout_pair((0, 1, depth - 2, depth - 1))
 
@@ -249,7 +257,6 @@
         for copy in down:
             copy.start()
 
-    middle = depth // 2
     relayout_pair(range(2, depth - 2))
 
     def inner_pair(group, carry):
@@ -548,8 +555,8 @@
             pltpu.SemaphoreType.DMA((6,)),
             pltpu.SemaphoreType.DMA((2, 2)),
             pltpu.SemaphoreType.DMA((2, 2)),
-            pltpu.SemaphoreType.DMA((halves - 1, 10)),
-            pltpu.SemaphoreType.DMA((halves - 1, 10)),
+            pltpu.SemaphoreType.DMA((halves - 1, 11)),
+            pltpu.SemaphoreType.DMA((halves - 1, 11)),
             pltpu.SemaphoreType.DMA((halves - 1,)),
             pltpu.SemaphoreType.DMA((1,)),
             pltpu.SemaphoreType.DMA((1,)),

time: 42.8 us -> 42.8 us (level)
  no operation moved by 1% of the time
where the time goes in v3:
time: 42.8 us; the launch traced here: 42.6 us
  Pallas kernels  42 us (98%)
  between operations  0.64 us (1%)
    pallas_call x1, Pallas kernels, on_device(): pl.pallas_call(functools.partial(kernel, slabs, halves), out_shape=(pltpu...  40.8 us
    pallas_call x1, Pallas kernels, on_device(): pl.pallas_call(write_back, out_shape=(jax.ShapeDtypeStruct(hc.shape, jnp....  1.19 us

profile of v3, /device:TPU:0, one launch (start us, length us, event | category | flops | bytes accessed | tf_op | source)
XLA Modules:
  0.0 42.6 jit_solution(11834980341208580145)
XLA Ops:
  0.6 40.8 %shard_map.77 = (f32[2048,128]{1,0:T(8,128)S(1)}, f32[1024,128]{1,0:T(8,128)S(1)}) custom-call(f32[2048,128]{1,0:T(8,128)} %bitcast.4, f32[1024,128]{1,0:T(8,128)} %bitcast.5, s32[16,128]{1,0:T(8,128)} %phase_ref.1, s32[16]{0:T(128)} %cell_ref.1, f32[16]{0:T(128)} %datum_ref.1, f32[16]{0:T(128)} %deviate_ref.1), custom_call_target="tpu_custom_call" | custom-call | tf_op jit(solution)/shard_map/pallas_call | solution.py:531
  41.4 1.2 %shard_map.78 = (f32[2048,128]{1,0:T(8,128)}, f32[1024,128]{1,0:T(8,128)}) custom-call(f32[2048,128]{1,0:T(8,128)S(1)} %get-tuple-element.6.hc, f32[1024,128]{1,0:T(8,128)S(1)} %get-tuple-element.7.vel), custom_call_target="tpu_custom_call" | custom-call | tf_op jit(solution)/shard_map/pallas_call | solution.py:583
